TPU v7x, 32 devices: a whole 2x2x4 slice. The times are simulated.
32 devices in a mesh: rep: 2 (over y), expert: 8 (over z, x), group: 2 (over core).
Axes of the slice: x: 2, y: 2, z: 4, core: 2. Of those that a mesh axis runs over, the one named last changes fastest.
Arguments:
- tokens: bfloat16 [4096, 1024], P(('rep', 'expert', 'group')), parts along dimension 0, may hold values from -6 to 6
- w_gate: bfloat16 [16, 1024, 384], P('expert', 'group'), may hold values from -0.1875 to 0.1875
- w_up: bfloat16 [16, 1024, 384], P('expert', 'group'), may hold values from -0.1875 to 0.1875
- w_down: bfloat16 [16, 384, 1024], P('expert', 'group'), may hold values from -0.45927933 to 0.45927933
- route_ids: int32 [4096, 8], P(('rep', 'expert', 'group')), parts along dimension 0, may hold values from 0 to 15, all different within a row; in each aligned block of 128 rows (0 to 127, 128 to 255, ...) at most 80 rows name the same one
- route_scores: float32 [4096, 8], P(('rep', 'expert', 'group')), parts along dimension 0, may hold values from 0.05 to 1
- norm_gain: float32 [1024], replicated, may hold values from 0.5 to 1.5
- class_head: bfloat16 [1024, 2000], P(None, 'expert'), may hold values from -0.59765625 to 0.59765625
- targets: int32 [16, 2, 2000], P('rep', 'group', 'expert'), parts along dimension 0, may hold values 0 or 1
Outputs:
- token_grad: bfloat16 [4096, 1024], P(('rep', 'expert', 'group')), parts along dimension 0
- head_grad: float32 [2048, 2000], P('rep', 'expert'), parts along dimension 0
There are 2 independent parts, one for each index of `rep`. A program takes and returns all parts, laid end to end along the dimension named above; an argument that names none is the same for every part. Nothing has to cross between parts.
Inputs may be any that keep to these rules, and one draw needn't show every extreme that they name: `route_ids`: each row names 8 different experts; among the 128 tokens of one sequence no expert is named by more than 80 tokens, and in some sequences one expert is named by exactly 80.
All inputs are finite; a program needn't handle non-finite values. No bound on the sum of `targets` on one device may be relied on, other than what follows from the above.
Results may differ from a plain program's by a relative error of at most 0.022.
Values may be sent and summed in bfloat16 or wider, within the bound.
A program may use at most 64 MiB of HBM per device.

v0:
```python
import jax
import jax.numpy as jnp
from jax import lax
from jax.sharding import PartitionSpec as P

LOSS_SCALE = 8.0
NORM_EPS = 1e-06


def body(tokens, w_gate, w_up, w_down, route_ids, route_scores, norm_gain, class_head, targets):
    rows_here, feature_dim = tokens.shape
    top_count = route_ids.shape[1]
    expert_count = lax.axis_size("expert")
    local_experts = w_gate.shape[0]
    experts_all = expert_count * local_experts
    capacity = min(rows_here, rows_here * top_count * 5 // (4 * experts_all))
    route_weight = route_scores / jnp.sum(route_scores, axis=-1, keepdims=True)
    expert_iota = jnp.arange(experts_all, dtype=jnp.int32)
    named_count = jnp.zeros((rows_here, experts_all), jnp.int32)
    for choice_k in range(top_count):
        named_count = named_count + (
            route_ids[:, choice_k][:, None] == expert_iota[None, :]
        ).astype(jnp.int32)
    before = jnp.cumsum(named_count, axis=0) - named_count
    position_cols = []
    for choice_k in range(top_count):
        hit_expert = route_ids[:, choice_k][:, None] == expert_iota[None, :]
        position_cols.append(jnp.sum(jnp.where(hit_expert, before, 0), axis=1))
    position = jnp.stack(position_cols, axis=1)
    slot_index = route_ids * capacity + position
    slot_iota = jnp.arange(experts_all * capacity, dtype=jnp.int32)
    place_rows = jnp.zeros((experts_all * capacity, rows_here), jnp.float32)
    place_weight = jnp.zeros((experts_all * capacity, rows_here), jnp.float32)
    for choice_k in range(top_count):
        slot_hit = slot_iota[:, None] == slot_index[:, choice_k][None, :]
        place_rows = place_rows + slot_hit.astype(jnp.float32)
        place_weight = place_weight + jnp.where(slot_hit, route_weight[:, choice_k][None, :], 0.0)
    place_rows = place_rows.astype(jnp.bfloat16)
    slot_shape = (expert_count, local_experts, capacity, feature_dim)
    outgoing = (
        jnp.dot(place_rows, tokens, preferred_element_type=jnp.float32)
        .astype(jnp.bfloat16)
        .reshape(slot_shape)
    )
    gate_full, up_full, down_full = (
        lax.all_gather(w_gate, "group", axis=1, tiled=True),
        lax.all_gather(w_up, "group", axis=1, tiled=True),
        lax.all_gather(w_down, "group", axis=1, tiled=True),
    )
    incoming = lax.all_to_all(outgoing, "expert", split_axis=0, concat_axis=0, tiled=True)
    gate_list = []
    up_list = []
    hidden_list = []
    for local in range(local_experts):
        expert_rows = incoming[:, local].reshape(-1, feature_dim)
        gate_act = jnp.dot(expert_rows, gate_full[local], preferred_element_type=jnp.float32)
        up_act = jnp.dot(expert_rows, up_full[local], preferred_element_type=jnp.float32)
        hidden = (gate_act * jax.nn.sigmoid(gate_act) * up_act).astype(jnp.bfloat16)
        gate_list.append(gate_act)
        up_list.append(up_act)
        hidden_list.append(hidden)
    out_list = []
    for local in range(local_experts):
        expert_out = jnp.dot(
            hidden_list[local], down_full[local], preferred_element_type=jnp.float32
        ).astype(jnp.bfloat16)
        out_list.append(expert_out.reshape(expert_count, capacity, feature_dim))
    expert_out_all = jnp.stack(out_list, axis=1)
    returned = lax.all_to_all(
        expert_out_all, "expert", split_axis=0, concat_axis=0, tiled=True
    ).reshape(-1, feature_dim)
    picked = jnp.take(returned, slot_index.reshape(-1), axis=0).reshape(
        rows_here, top_count, feature_dim
    )
    moe_out = jnp.einsum("tk,tkd->td", route_weight, picked.astype(jnp.float32))
    residual = tokens.astype(jnp.float32) + moe_out
    inv_rms = lax.rsqrt(jnp.mean(residual * residual, axis=-1, keepdims=True) + NORM_EPS)
    normed = residual * inv_rms * norm_gain
    pooled = jnp.mean(normed, axis=0, keepdims=True).astype(jnp.bfloat16)
    pooled_all = lax.all_gather(pooled, "expert", axis=0, tiled=True)
    logits = jnp.dot(pooled_all, class_head, preferred_element_type=jnp.float32)
    target_rows = targets.reshape(expert_count, -1).astype(jnp.float32)
    logit_grad = (LOSS_SCALE * (jax.nn.sigmoid(logits) - target_rows)).astype(jnp.bfloat16)
    head_part = lax.dot_general(
        pooled_all, logit_grad, (((0,), (0,)), ((), ())), preferred_element_type=jnp.float32
    )
    head_grad = lax.psum(head_part.astype(jnp.bfloat16), "group").astype(jnp.float32)
    pooled_terms = lax.dot_general(
        logit_grad, class_head, (((1,), (1,)), ((), ())), preferred_element_type=jnp.float32
    )
    pooled_grad = lax.psum_scatter(
        pooled_terms.astype(jnp.bfloat16), "expert", scatter_dimension=0, tiled=True
    ).astype(jnp.float32)
    scaled = norm_gain * pooled_grad / rows_here
    cube = inv_rms * inv_rms * inv_rms
    resid_grad = inv_rms * scaled - residual * cube * jnp.mean(
        residual * scaled, axis=-1, keepdims=True
    )
    slot_grad = jnp.dot(
        place_weight,
        resid_grad,
        precision=lax.Precision.HIGHEST,
        preferred_element_type=jnp.float32,
    )
    slot_grad = slot_grad.astype(jnp.bfloat16).reshape(slot_shape)
    grad_in = lax.all_to_all(slot_grad, "expert", split_axis=0, concat_axis=0, tiled=True)
    back_list = []
    for local in range(local_experts):
        grad_rows = grad_in[:, local].reshape(-1, feature_dim)
        gate_act = gate_list[local]
        sigmoid_gate = jax.nn.sigmoid(gate_act)
        down_back = lax.dot_general(
            grad_rows,
            down_full[local],
            (((1,), (1,)), ((), ())),
            preferred_element_type=jnp.float32,
        )
        silu_slope = sigmoid_gate * (1.0 + gate_act * (1.0 - sigmoid_gate))
        gate_grad = (down_back * up_list[local] * silu_slope).astype(jnp.bfloat16)
        up_grad = (down_back * gate_act * sigmoid_gate).astype(jnp.bfloat16)
        input_grad = lax.dot_general(
            gate_grad,
            gate_full[local],
            (((1,), (1,)), ((), ())),
            preferred_element_type=jnp.float32,
        )
        input_grad = input_grad + lax.dot_general(
            up_grad, up_full[local], (((1,), (1,)), ((), ())), preferred_element_type=jnp.float32
        )
        back_list.append(
            input_grad.astype(jnp.bfloat16).reshape(expert_count, capacity, feature_dim)
        )
    input_grad_all = jnp.stack(back_list, axis=1)
    grad_back = lax.all_to_all(
        input_grad_all, "expert", split_axis=0, concat_axis=0, tiled=True
    ).reshape(-1, feature_dim)
    grad_pick = jnp.take(grad_back, slot_index.reshape(-1), axis=0).reshape(
        rows_here, top_count, feature_dim
    )
    token_grad = (resid_grad + jnp.sum(grad_pick.astype(jnp.float32), axis=1)).astype(jnp.bfloat16)
    return (token_grad, head_grad)


def solution(mesh):
    in_specs = (
        P(("rep", "expert", "group"), None),
        P("expert", "group", None),
        P("expert", "group", None),
        P("expert", "group", None),
        P(("rep", "expert", "group"), None),
        P(("rep", "expert", "group"), None),
        P(),
        P(None, "expert"),
        P("rep", "group", "expert"),
    )
    out_specs = (P(("rep", "expert", "group"), None), P("rep", "expert"))
    return jax.shard_map(body, mesh=mesh, in_specs=in_specs, out_specs=out_specs, check_vma=False)
```

profile of v0, /device:TPU:0, one launch (start us, length us, event | category | flops | bytes accessed | tf_op | source)
XLA Modules:
  0.0 371.7 jit_solution(3693473801401391951)
XLA Ops:
  7.2 1.0 slice_bitcast_fusion.41
  8.2 0.2 convert_add_fusion
  8.4 0.2 reduce_window_sum.11
  8.5 0.4 select_reduce_fusion
  9.0 0.7 multiply_add_fusion
  9.7 3.5 convolution_convert_fusion.1
  13.2 7.2 %all-to-all-start = ((bf16[8,2,80,1024]{3,2,1,0:T(8,128)(2,1)}), bf16[8,2,80,1024]{3,2,1,0:T(8,128)(2,1)S(1)}, u32[]{:S(2)}, u32[]{:S(2)}) async-start(bf16[8,2,80,1024]{3,2,1,0:T(8,128)(2,1)} %bitcast.142), calls=%async_computation | async-start | bytes 5242880 | tf_op jit(solution)/shard_map/all_to_all | solution.py:50
  20.4 0.0 all-gather.5.cloned.1.call-start
  20.5 0.7 all-gather.5.cloned.1.call-update
  21.2 0.0 all-gather.7.cloned.1.call-start
  21.2 0.7 all-gather.7.cloned.1.call-update
  21.9 0.0 all-gather.9.cloned.1.call-start
  22.0 0.7 all-gather.9.cloned.1.call-update
  22.7 57.3 %all-to-all-done = bf16[8,2,80,1024]{3,2,1,0:T(8,128)(2,1)S(1)} async-done(((bf16[8,2,80,1024]{3,2,1,0:T(8,128)(2,1)}), bf16[8,2,80,1024]{3,2,1,0:T(8,128)(2,1)S(1)}, u32[]{:S(2)}, u32[]{:S(2)}) %all-to-all-start) | async-done | bytes 2621472 | tf_op jit(solution)/shard_map/all_to_all | solution.py:50
  79.9 1.9 fusion.82
  81.8 3.4 fusion.12
  85.2 3.1 fusion.13
  88.3 1.9 fusion.17
  90.2 0.8 fusion.16
  91.0 0.0 all-gather.9.cloned.1.call-done
  91.1 3.0 convolution_convert_fusion.3
  94.1 0.9 convolution_convert_fusion.2
  95.0 1.7 pad_maximum_fusion
  96.7 3.8 %all-to-all-start.1 = ((bf16[8,2,80,1024]{3,2,1,0:T(8,128)(2,1)}), bf16[8,2,80,1024]{3,2,1,0:T(8,128)(2,1)S(1)}, u32[]{:S(2)}, u32[]{:S(2)}) async-start(bf16[8,2,80,1024]{3,2,1,0:T(8,128)(2,1)} %pad_maximum_fusion), calls=%async_computation.1 | async-start | bytes 5242880 | tf_op jit(solution)/shard_map/all_to_all | solution.py:69
  100.5 0.1 copy.18
  100.6 0.1 reshape.86
  100.7 0.1 copy.24
  100.9 0.6 dynamic-slice
  101.5 58.6 %all-to-all-done.1 = bf16[8,2,80,1024]{3,2,1,0:T(8,128)(2,1)S(1)} async-done(((bf16[8,2,80,1024]{3,2,1,0:T(8,128)(2,1)}), bf16[8,2,80,1024]{3,2,1,0:T(8,128)(2,1)S(1)}, u32[]{:S(2)}, u32[]{:S(2)}) %all-to-all-start.1) | async-done | bytes 2621472 | tf_op jit(solution)/shard_map/all_to_all | solution.py:69
  160.1 5.4 %gather_fusion = bf16[1024,1024]{1,0:T(8,128)(2,1)} fusion(bf16[1280,1024]{1,0:T(8,128)(2,1)S(1)} %bitcast.140, s32[1024]{0:T(1024)S(1)} %fusion.71), kind=kCustom, calls=%fused_computation.clone | custom fusion | bytes 4198400 | tf_op jit(solution)/shard_map/jit(_take)/gather | solution.py:72
  165.5 2.4 fusion
  167.9 0.2 multiply_reduce_fusion.2
  168.1 0.2 multiply_reduce_fusion.1
  168.3 26.0 %all-gather = bf16[8192]{0:T(1024)(128)(2,1)S(1)} all-gather(bf16[1024]{0:T(1024)(128)(2,1)S(1)} %multiply_convert_fusion.12), channel_id=2, replica_groups=mesh['rep'=2,'expert'=8,'group'=2] {'expert'}, dimensions={0}, use_global_device_ids=true | all-gather | bytes 18432 | tf_op jit(solution)/shard_map/all_gather | solution.py:80
  194.3 0.2 fusion.9
  194.5 0.2 convolution_convert_fusion.5
  194.8 33.8 %all-reduce = bf16[8,1024]{1,0:T(8,128)(2,1)S(1)} all-reduce(bf16[8,1024]{1,0:T(8,128)(2,1)S(1)} %convolution_convert_fusion.5), channel_id=3, replica_groups=mesh['rep'=2,'expert'=8,'group'=2] {'expert'}, use_global_device_ids=true, to_apply=%region_12.14.clone | all-reduce | flops 8192 | bytes 32768
  228.5 0.7 fusion.70
  229.2 0.2 multiply_reduce_fusion
  229.4 5.3 %convolution_convert_fusion = bf16[1280,1024]{1,0:T(8,128)(2,1)S(1)} fusion(f32[128]{0:T(128)S(1)} %get-tuple-element.16, f32[128]{0:T(128)S(1)} %get-tuple-element.17, f32[128]{0:T(128)S(1)} %get-tuple-element.18, f32[128]{0:T(128)S(1)} %get-tuple-element.19, f32[128]{0:T(128)S(1)} %get-tuple-element.20, f32[128]{0:T(128)S(1)} %get-tuple-element.21, ...), kind=kOutput, calls=%fused_computation.3 | convolution fusion | flops 2019131392 | bytes 3421696 | tf_op jit(solution)/shard_map/dot_general | solution.py:99
  234.7 51.1 %all_to_all.20 = bf16[8,2,80,1024]{3,2,1,0:T(8,128)(2,1)S(1)} all-to-all(bf16[8,2,80,1024]{3,2,1,0:T(8,128)(2,1)S(1)} %bitcast.143), channel_id=1, replica_groups=mesh['rep'=2,'expert'=8,'group'=2] {'expert'}, dimensions={0} | all-to-all | bytes 5242880 | tf_op jit(solution)/shard_map/all_to_all | solution.py:106
  285.8 0.4 fusion.81
  286.2 1.0 copy-done.14
  287.2 0.9 fusion.14
  288.1 0.6 copy-done.10
  288.7 0.3 copy-done.20
  288.9 1.0 fusion.11
  290.0 0.4 copy-done.12
  290.4 0.9 add_convert_fusion.1
  291.3 0.9 fusion.18
  292.2 0.3 copy-done.17
  292.5 0.3 copy-done.19
  292.8 1.0 fusion.15
  293.8 0.9 add_convert_fusion
  294.7 1.7 pad_maximum_fusion.1
  296.5 3.7 all-to-all-start.3
  300.1 0.0 all-reduce.3.cloned.1.call-start
  300.2 1.1 convolution_convert_fusion.4
  301.4 22.4 %all-reduce.3.cloned.1.call-done = bf16[1024,250]{1,0:T(8,128)(2,1)} async-done(((bf16[1024,250]{1,0:T(8,128)(2,1)}), bf16[1024,250]{1,0:T(8,128)(2,1)}) %all-reduce.3.cloned.1.call-update) | async-done | bytes 512016 | tf_op jit(solution)/shard_map/psum | solution.py:87
  323.8 2.1 convert_element_type.176
  325.9 30.0 %all-to-all-done.3 = bf16[8,2,80,1024]{3,2,1,0:T(8,128)(2,1)S(1)} async-done(((bf16[8,2,80,1024]{3,2,1,0:T(8,128)(2,1)}), bf16[8,2,80,1024]{3,2,1,0:T(8,128)(2,1)S(1)}, u32[]{:S(2)}, u32[]{:S(2)}) %all-to-all-start.3) | async-done | bytes 2621472 | tf_op jit(solution)/shard_map/all_to_all | solution.py:134
  355.9 5.4 %gather_fusion.1 = bf16[1024,1024]{1,0:T(8,128)(2,1)} fusion(bf16[1280,1024]{1,0:T(8,128)(2,1)S(1)} %bitcast.141, s32[1024]{0:T(1024)S(1)} %fusion.71), kind=kCustom, calls=%fused_computation.1.clone | custom fusion | bytes 4198400 | tf_op jit(solution)/shard_map/jit(_take)/gather | solution.py:137
  361.2 3.0 convert_reduce_fusion
  364.3 0.9 add_convert_fusion.3
  (53 shorter events, 0.2 us)
Async XLA Ops:
  7.2 187.2 %copy-start = (bf16[1024,250]{1,0:T(8,128)(2,1)S(1)}, bf16[1024,250]{1,0:T(8,128)(2,1)}, u32[]{:S(2)}) copy-start(bf16[1024,250]{1,0:T(8,128)(2,1)} %param.18) | copy-start | bytes 1536004
  13.2 66.7 %all-to-all-start = ((bf16[8,2,80,1024]{3,2,1,0:T(8,128)(2,1)}), bf16[8,2,80,1024]{3,2,1,0:T(8,128)(2,1)S(1)}, u32[]{:S(2)}, u32[]{:S(2)}) async-start(bf16[8,2,80,1024]{3,2,1,0:T(8,128)(2,1)} %bitcast.142), calls=%async_computation | async-start | bytes 5242880 | tf_op jit(solution)/shard_map/all_to_all | solution.py:50
  20.4 61.4 %all-gather.5.cloned.1.call-start = ((), (), s32[]{:S(2)}) async-start(), calls=%async_computation.4 | async-start | bytes 2359296 | tf_op jit(solution)/shard_map/all_gather | solution.py:46
  21.2 64.1 %all-gather.7.cloned.1.call-start = ((), (), s32[]{:S(2)}) async-start(), calls=%async_computation.5 | async-start | bytes 2359296 | tf_op jit(solution)/shard_map/all_gather | solution.py:47
  21.9 69.1 %all-gather.9.cloned.1.call-start = ((), (), s32[]{:S(2)}) async-start(), calls=%async_computation.6 | async-start | bytes 2359296 | tf_op jit(solution)/shard_map/all_gather | solution.py:48
  81.8 3.4 copy-start.5
  85.2 3.1 copy-start.4
  85.2 3.1 copy-start.11
  88.3 1.9 copy-start.9
  91.0 3.0 copy-start.16
  91.0 3.0 copy-start.18
  91.1 3.0 copy-start.13
  96.7 4.0 %copy-start.6 = (f32[128,8]{0,1:T(8,128)S(1)}, f32[128,8]{0,1:T(8,128)}, u32[]{:S(2)}) copy-start(f32[128,8]{0,1:T(8,128)} %param.16) | copy-start | bytes 12292
  96.7 4.2 %copy-start.15 = (u32[32]{0:T(128)S(1)}, u32[32]{0:T(128)}, u32[]{:S(2)}) copy-start(u32[32]{0:T(128)} %constant.41) | copy-start | bytes 388
  96.7 63.4 %all-to-all-start.1 = ((bf16[8,2,80,1024]{3,2,1,0:T(8,128)(2,1)}), bf16[8,2,80,1024]{3,2,1,0:T(8,128)(2,1)S(1)}, u32[]{:S(2)}, u32[]{:S(2)}) async-start(bf16[8,2,80,1024]{3,2,1,0:T(8,128)(2,1)} %pad_maximum_fusion), calls=%async_computation.1 | async-start | bytes 5242880 | tf_op jit(solution)/shard_map/all_to_all | solution.py:69
  165.5 2.4 copy-start.3
  165.5 2.6 copy-start.7
  167.9 61.5 %copy-start.1 = (f32[128,1,1024]{2,1,0:T(1,128)}, f32[128,1,1024]{2,1,0:T(1,128)S(1)}, u32[]{:S(2)}) copy-start(f32[128,1,1024]{2,1,0:T(1,128)S(1)} %fusion) | copy-start | bytes 1572868
  167.9 26.4 %copy-start.8 = (s32[8,1,250]{2,1,0:T(1,128)S(1)}, s32[8,1,250]{2,1,0:T(1,128)}, u32[]{:S(2)}) copy-start(s32[8,1,250]{2,1,0:T(1,128)} %param.19) | copy-start | bytes 24004
  285.8 1.4 copy-start.14
  285.8 2.3 copy-start.21
  287.2 1.5 copy-start.10
  287.2 1.7 copy-start.20
  288.9 1.4 copy-start.12
  291.3 1.2 copy-start.17
  291.3 1.5 copy-start.19
  296.5 59.4 %all-to-all-start.3 = ((bf16[8,2,80,1024]{3,2,1,0:T(8,128)(2,1)}), bf16[8,2,80,1024]{3,2,1,0:T(8,128)(2,1)S(1)}, u32[]{:S(2)}, u32[]{:S(2)}) async-start(bf16[8,2,80,1024]{3,2,1,0:T(8,128)(2,1)} %pad_maximum_fusion.1), calls=%async_computation.3 | async-start | bytes 5242880 | tf_op jit(solution)/shard_map/all_to_all | solution.py:134
  300.1 23.6 %all-reduce.3.cloned.1.call-start = ((), (), s32[]{:S(2)}) async-start(), calls=%async_computation.7 | async-start | bytes 1048576 | tf_op jit(solution)/shard_map/psum | solution.py:87
  361.2 3.0 copy-start.2
Sparse Core Ops, SparseCore 0:
  22.8 11.2 all-gather.4
  35.6 10.9 all-gather.6
  48.2 10.9 all-gather.8
  303.6 20.1 all-reduce.2
where the time goes:
time: 372 us
  waiting for transfers between devices  170 us (46%)
  blocking collectives  111 us (30%)
  matrix products  31.4 us (8%)
  local copies, waits for them, and re-layouts  17.9 us (5%)
  starting transfers between devices  14.8 us (4%)
  between operations  14.1 us (4%)
  other arithmetic  12.2 us (3%)
    all_to_all x1, waiting for transfers between devices, body(): lax.all_to_all(expert_out_all, 'expert', split_axis=0, concat_axis=0, til...  58.6 us
    all_to_all x1, waiting for transfers between devices, body(): lax.all_to_all(outgoing, 'expert', split_axis=0, concat_axis=0, tiled=True)  57.3 us
    all_to_all x1, blocking collectives, body(): lax.all_to_all(slot_grad, 'expert', split_axis=0, concat_axis=0, tiled=True)  51.1 us
    unnamed x1, blocking collectives  33.8 us
    all_to_all x1, waiting for transfers between devices, body(): lax.all_to_all(input_grad_all, 'expert', split_axis=0, concat_axis=0, til...  30 us
    all_gather x1, blocking collectives, body(): pooled_all = lax.all_gather(pooled, 'expert', axis=0, tiled=True)  26 us
    psum x1, waiting for transfers between devices, body(): lax.psum(head_part.astype(jnp.bfloat16), 'group').astype(jnp.float32)  22.4 us
  transfers between devices with their start and end apart: 7, of which 4 were waited for; matrix products, arithmetic and copies ran while one was open for 4% of the time, Pallas kernels for 0%

commit v1 on v0

v1 whole, which is shorter than its diff:
```python
import functools

import jax
import jax.numpy as jnp
from jax import lax
from jax.experimental import pallas as pl
from jax.experimental.pallas import tpu as pltpu
from jax.sharding import PartitionSpec as P

LOSS_SCALE = 8.0
NORM_EPS = 1e-06
LANES = 128
HALF = 64
NT = (((1,), (1,)), ((), ()))


def ring_place(expert, n, snake):
    if not snake:
        return expert
    odd = lax.rem(expert, 2)
    return (1 - odd) * (expert // 2) + odd * (n - 1 - expert // 2)


def ring_expert(place, n, snake):
    if not snake:
        return place
    back = place // (n // 2)
    return (1 - back) * 2 * place + back * (2 * n - 1 - 2 * place)


def kernel(
    n,
    groups,
    gather_weights,
    snake,
    tok_ref,
    ids_ref,
    score_ref,
    gain_ref,
    head_ref,
    target_ref,
    wg_ref,
    wu_ref,
    wd_ref,
    out_ref,
    pool_ref,
    lg_ref,
    wg,
    wu,
    wd,
    xbuf,
    gbuf,
    gate_coef,
    up_coef,
    part,
    from_right,
    from_left,
    resid,
    pool_mine,
    pool_all,
    terms,
    terms_in,
    w_local_sem,
    w_send_sem,
    w_recv_sem,
    cw_send,
    ccw_send,
    ring_recv,
    left_send,
    right_send,
    left_recv,
    right_recv,
    small_send,
    small_recv,
    group_send,
    group_recv,
):
    rows, width = tok_ref.shape
    local, _, hidden = wg.shape
    half = n // 2
    expert = lax.axis_index("expert")
    group = lax.axis_index("group")
    place = ring_place(expert, n, snake)
    right = ring_expert(lax.rem(place + 1, n), n, snake)
    left = ring_expert(lax.rem(place + n - 1, n), n, snake)

    barrier = pltpu.get_barrier_semaphore()
    for off in range(1, n):
        pl.semaphore_signal(barrier, inc=1, device_id={"expert": lax.rem(expert + off, n)})
    for off in range(1, groups):
        pl.semaphore_signal(barrier, inc=1, device_id={"group": lax.rem(group + off, groups)})

    locals_ = []
    for i, (src, dst) in enumerate(((wg_ref, wg), (wu_ref, wu), (wd_ref, wd))):
        span = src.shape[1]
        at = pl.multiple_of(group * span, 16) if gather_weights else 0
        copy = pltpu.make_async_copy(src, dst.at[:, pl.ds(at, span), :], w_local_sem.at[i])
        copy.start()
        locals_.append(copy)

    ids = ids_ref[...]
    score = score_ref[...]
    weight = score / jnp.sum(score, axis=-1, keepdims=True)
    lane = lax.rem(lax.broadcasted_iota(jnp.int32, (rows, LANES), 1), HALF)
    low = lax.broadcasted_iota(jnp.int32, (rows, LANES), 1) < HALF
    by_expert = jnp.zeros((rows, LANES), jnp.float32)
    for k in range(ids.shape[1]):
        by_expert += jnp.where(lane == ids[:, k : k + 1], weight[:, k : k + 1], 0.0)
    high_part = by_expert.astype(jnp.bfloat16).astype(jnp.float32)
    xbuf[0, :, :width] = tok_ref[...]
    xbuf[0, :, width:] = jnp.where(low, high_part, by_expert - high_part).astype(jnp.bfloat16)

    pl.semaphore_wait(barrier, n - 1 + groups - 1)

    def cw(buf, phase, k):
        return pltpu.make_async_remote_copy(
            src_ref=buf.at[k],
            dst_ref=buf.at[k + 1],
            send_sem=cw_send.at[phase, k],
            recv_sem=ring_recv.at[phase, k + 1],
            device_id={"expert": right},
        )

    def ccw(buf, phase, k):
        return pltpu.make_async_remote_copy(
            src_ref=buf.at[lax.rem(k, n)],
            dst_ref=buf.at[k - 1],
            send_sem=ccw_send.at[phase, k - 1],
            recv_sem=ring_recv.at[phase, k - 1],
            device_id={"expert": left},
        )

    cw(xbuf, 0, 0).start()
    ccw(xbuf, 0, n).start()

    w_copies = []
    if gather_weights:
        for off in range(1, groups):
            for i, (src, dst) in enumerate(((wg_ref, wg), (wu_ref, wu), (wd_ref, wd))):
                span = src.shape[1]
                at = pl.multiple_of(group * span, 16)
                copy = pltpu.make_async_remote_copy(
                    src_ref=src,
                    dst_ref=dst.at[:, pl.ds(at, span), :],
                    send_sem=w_send_sem.at[off, i],
                    recv_sem=w_recv_sem.at[off, i],
                    device_id={"group": lax.rem(group + off, groups)},
                )
                copy.start()
                w_copies.append(copy)
    for copy in locals_:
        copy.wait()
    for copy in w_copies:
        copy.wait()

    def forward_block(k):
        x = xbuf[k, :, :width]
        ext = xbuf[k, :, width:].astype(jnp.float32)
        total = jnp.zeros((rows, width), jnp.float32)
        for j in range(local):
            w = jnp.sum(jnp.where(lane == expert * local + j, ext, 0.0), axis=1, keepdims=True)
            gate = jnp.dot(x, wg[j], preferred_element_type=jnp.float32)
            up = jnp.dot(x, wu[j], preferred_element_type=jnp.float32)
            sig = 1.0 / (1.0 + jnp.exp(-gate))
            silu = gate * sig * w
            gate_coef[k, j] = up * (sig * (1.0 + gate * (1.0 - sig))) * w
            up_coef[k, j] = silu
            total += jnp.dot(
                (silu * up).astype(jnp.bfloat16), wd[j], preferred_element_type=jnp.float32
            )
        part[0, k] = total.astype(jnp.bfloat16)

    def backward_block(k):
        g = gbuf[k]
        total = jnp.zeros((rows, width), jnp.float32)
        for j in range(local):
            back = lax.dot_general(g, wd[j], NT, preferred_element_type=jnp.float32)
            gate_grad = (back * gate_coef[k, j]).astype(jnp.bfloat16)
            up_grad = (back * up_coef[k, j]).astype(jnp.bfloat16)
            total += lax.dot_general(gate_grad, wg[j], NT, preferred_element_type=jnp.float32)
            total += lax.dot_general(up_grad, wu[j], NT, preferred_element_type=jnp.float32)
        part[1, k] = total.astype(jnp.bfloat16)

    def gather_phase(buf, phase, block):
        def step(i, carry):
            s = (i + 1) // 2
            odd = lax.rem(i, 2)

            @pl.when(odd == 1)
            def _():
                cw(buf, phase, s - 1).wait_recv()

                @pl.when(s < half)
                def _():
                    cw(buf, phase, s).start()
                    ccw(buf, phase, n - s + 1).wait_recv()

                    @pl.when(s < half - 1)
                    def _():
                        ccw(buf, phase, n - s).start()

            block(odd * s + (1 - odd) * lax.rem(n - s, n))
            return carry

        lax.fori_loop(0, n, step, 0)

        def drain_cw(k, carry):
            cw(buf, phase, k).wait_send()
            return carry

        def drain_ccw(k, carry):
            ccw(buf, phase, n - k).wait_send()
            return carry

        lax.fori_loop(0, half, drain_cw, 0)
        lax.fori_loop(0, half - 1, drain_ccw, 0)

    def to_left(phase, k):
        return pltpu.make_async_remote_copy(
            src_ref=part.at[phase, k],
            dst_ref=from_right.at[phase, k - 1],
            send_sem=left_send.at[phase, k],
            recv_sem=left_recv.at[phase, k - 1],
            device_id={"expert": left},
        )

    def to_right(phase, d):
        return pltpu.make_async_remote_copy(
            src_ref=part.at[phase, n - d],
            dst_ref=from_left.at[phase, d - 1],
            send_sem=right_send.at[phase, d],
            recv_sem=right_recv.at[phase, d - 1],
            device_id={"expert": right},
        )

    def reduce_phase(phase):
        to_left(phase, half).start()
        to_right(phase, half - 1).start()

        def step(s, carry):
            k = half - s
            to_left(phase, k + 1).wait_recv()
            part[phase, k] = (
                part[phase, k].astype(jnp.float32) + from_right[phase, k].astype(jnp.float32)
            ).astype(jnp.bfloat16)
            to_left(phase, k).start()

            @pl.when(s < half - 1)
            def _():
                d = half - 1 - s
                to_right(phase, d + 1).wait_recv()
                part[phase, n - d] = (
                    part[phase, n - d].astype(jnp.float32)
                    + from_left[phase, d].astype(jnp.float32)
                ).astype(jnp.bfloat16)
                to_right(phase, d).start()

            return carry

        lax.fori_loop(1, half, step, 0)
        to_right(phase, 1).wait_recv()
        to_left(phase, 1).wait_recv()

        def drain_left(k, carry):
            to_left(phase, k).wait_send()
            return carry

        def drain_right(d, carry):
            to_right(phase, d).wait_send()
            return carry

        lax.fori_loop(1, half + 1, drain_left, 0)
        lax.fori_loop(1, half, drain_right, 0)
        return (
            part[phase, 0].astype(jnp.float32)
            + from_right[phase, 0].astype(jnp.float32)
            + from_left[phase, 0].astype(jnp.float32)
        )

    gather_phase(xbuf, 0, forward_block)
    residual = xbuf[0, :, :width].astype(jnp.float32) + reduce_phase(0)
    gain = gain_ref[...]
    inv_rms = lax.rsqrt(jnp.mean(residual * residual, axis=-1, keepdims=True) + NORM_EPS)
    resid[...] = residual
    pooled = jnp.sum(residual * inv_rms * gain, axis=0, keepdims=True) / rows
    pooled = pooled.astype(jnp.bfloat16).astype(jnp.float32)
    pool_mine[...] = pooled
    pool_all[pl.ds(expert, 1)] = pooled[None]

    def small(i, src, dst, off):
        return pltpu.make_async_remote_copy(
            src_ref=src,
            dst_ref=dst,
            send_sem=small_send.at[i, off],
            recv_sem=small_recv.at[i, off],
            device_id={"expert": lax.rem(expert + off, n)},
        )

    copies = [small(0, pool_mine, pool_all.at[expert], off) for off in range(1, n)]
    for copy in copies:
        copy.start()
    for copy in copies:
        copy.wait()
    pooled_rows = jnp.concatenate([pool_all[i] for i in range(n)], axis=0).astype(jnp.bfloat16)
    logits = jnp.dot(pooled_rows, head_ref[...], preferred_element_type=jnp.float32)
    sig = 1.0 / (1.0 + jnp.exp(-logits))
    logit_grad = (LOSS_SCALE * (sig - target_ref[...].astype(jnp.float32))).astype(jnp.bfloat16)
    pooled_terms = lax.dot_general(logit_grad, head_ref[...], NT, preferred_element_type=jnp.float32)
    for i in range(n):
        terms[i] = pooled_terms[i : i + 1, :]
    copies = [
        small(1, terms.at[lax.rem(expert + off, n)], terms_in.at[off], off) for off in range(1, n)
    ]
    for copy in copies:
        copy.start()
    pool_ref[pl.ds(group, 1)] = pooled_rows.astype(jnp.float32)[None]
    lg_ref[pl.ds(group, 1)] = logit_grad.astype(jnp.float32)[None]
    group_copies = []
    for off in range(1, groups):
        for i, ref in enumerate((pool_ref, lg_ref)):
            copy = pltpu.make_async_remote_copy(
                src_ref=ref.at[group],
                dst_ref=ref.at[group],
                send_sem=group_send.at[off, i],
                recv_sem=group_recv.at[off, i],
                device_id={"group": lax.rem(group + off, groups)},
            )
            copy.start()
            group_copies.append(copy)
    for copy in copies:
        copy.wait()
    pooled_grad = terms[expert]
    for off in range(1, n):
        pooled_grad = pooled_grad + terms_in[off]
    residual = resid[...]
    inv_rms = lax.rsqrt(jnp.mean(residual * residual, axis=-1, keepdims=True) + NORM_EPS)
    scaled = gain * pooled_grad / rows
    cube = inv_rms * inv_rms * inv_rms
    resid_grad = inv_rms * scaled - residual * (
        cube * jnp.mean(residual * scaled, axis=-1, keepdims=True)
    )
    gbuf[0] = resid_grad.astype(jnp.bfloat16)
    cw(gbuf, 1, 0).start()
    ccw(gbuf, 1, n).start()
    resid[...] = resid_grad
    gather_phase(gbuf, 1, backward_block)
    out_ref[...] = (resid[...] + reduce_phase(1)).astype(jnp.bfloat16)
    for copy in group_copies:
        copy.wait()


def body(tokens, w_gate, w_up, w_down, route_ids, route_scores, norm_gain, class_head, targets):
    rows, width = tokens.shape
    n = lax.axis_size("expert")
    groups = lax.axis_size("group")
    local, _, hidden = w_gate.shape
    labels = class_head.shape[1]
    half = n // 2
    gather_weights = w_gate.shape[1] % 16 == 0 and w_down.shape[1] % 16 == 0
    if not gather_weights:
        w_gate = lax.all_gather(w_gate, "group", axis=1, tiled=True)
        w_up = lax.all_gather(w_up, "group", axis=1, tiled=True)
        w_down = lax.all_gather(w_down, "group", axis=1, tiled=True)
    vmem = pl.BlockSpec(memory_space=pltpu.VMEM)
    hbm = pl.BlockSpec(memory_space=pl.ANY)
    dma = pltpu.SemaphoreType.DMA
    bf16, f32 = jnp.bfloat16, jnp.float32
    token_grad, pool, lg = pl.pallas_call(
        functools.partial(kernel, n, groups, gather_weights, n == 8),
        out_shape=(
            jax.ShapeDtypeStruct((rows, width), bf16),
            jax.ShapeDtypeStruct((groups, n, width), f32),
            jax.ShapeDtypeStruct((groups, n, labels), f32),
        ),
        in_specs=[vmem] * 6 + [hbm] * 3,
        out_specs=(vmem, vmem, vmem),
        scratch_shapes=[
            pltpu.VMEM((local, width, hidden), bf16),
            pltpu.VMEM((local, width, hidden), bf16),
            pltpu.VMEM((local, hidden, width), bf16),
            pltpu.VMEM((n, rows, width + LANES), bf16),
            pltpu.VMEM((n, rows, width), bf16),
            pltpu.VMEM((n, local, rows, hidden), f32),
            pltpu.VMEM((n, local, rows, hidden), f32),
            pltpu.VMEM((2, n, rows, width), bf16),
            pltpu.VMEM((2, half, rows, width), bf16),
            pltpu.VMEM((2, half, rows, width), bf16),
            pltpu.VMEM((rows, width), f32),
            pltpu.VMEM((1, width), f32),
            pltpu.VMEM((n, 1, width), f32),
            pltpu.VMEM((n, 1, width), f32),
            pltpu.VMEM((n, 1, width), f32),
            dma((3,)),
            dma((groups, 3)),
            dma((groups, 3)),
            dma((2, n)),
            dma((2, n)),
            dma((2, n)),
            dma((2, n)),
            dma((2, n)),
            dma((2, n)),
            dma((2, n)),
            dma((2, n)),
            dma((2, n)),
            dma((groups, 2)),
            dma((groups, 2)),
        ],
        compiler_params=pltpu.CompilerParams(
            collective_id=0, has_side_effects=True, vmem_limit_bytes=60 * 1024 * 1024
        ),
    )(
        tokens,
        route_ids,
        route_scores,
        norm_gain.reshape(1, width),
        class_head,
        targets.reshape(n, labels),
        w_gate,
        w_up,
        w_down,
    )
    head_grad = lax.dot_general(
        pool.reshape(-1, width).astype(bf16),
        lg.reshape(-1, labels).astype(bf16),
        (((0,), (0,)), ((), ())),
        preferred_element_type=f32,
    )
    return token_grad, head_grad


def solution(mesh):
    in_specs = (
        P(("rep", "expert", "group"), None),
        P("expert", "group", None),
        P("expert", "group", None),
        P("expert", "group", None),
        P(("rep", "expert", "group"), None),
        P(("rep", "expert", "group"), None),
        P(),
        P(None, "expert"),
        P("rep", "group", "expert"),
    )
    out_specs = (P(("rep", "expert", "group"), None), P("rep", "expert"))
    return jax.shard_map(body, mesh=mesh, in_specs=in_specs, out_specs=out_specs, check_vma=False)
```

time: 372 us -> 139 us (0.37)
  waiting for transfers between devices: 170 us -> 0 us
  Pallas kernels: 0 us -> 132 us
  blocking collectives: 111 us -> 0 us
  matrix products: 31.4 us -> 2.2 us
  starting transfers between devices: 14.8 us -> 0 us
  local copies, waits for them, and re-layouts: 17.9 us -> 3.47 us
  between operations: 14.1 us -> 0.66 us
  other arithmetic: 12.2 us -> 0 us
    all_to_all x3 -> x0, waiting for transfers between devices: 146 us -> none  [the longest x1 58.6 us: body(): lax.all_to_all(expert_out_all, 'expert', split_axis=0, concat_axis=0, til...]
    pallas_call x0 -> x1, Pallas kernels: none -> 132 us  [body(): pl.pallas_call(functools.partial(kernel, n, groups, gather_weights, n ==...]
    all_to_all x1 -> x0, blocking collectives: 51.1 us -> none  [body(): lax.all_to_all(slot_grad, 'expert', split_axis=0, concat_axis=0, tiled=True)]
    unnamed x1 -> x0, blocking collectives: 33.8 us -> none
    dot_general x18 -> x1, matrix products: 31.4 us -> 2.2 us  [body(): lax.dot_general(pool.reshape(-1, width).astype(bf16), lg.reshape(-1, labe...]
    all_gather x1 -> x0, blocking collectives: 26 us -> none  [body(): pooled_all = lax.all_gather(pooled, 'expert', axis=0, tiled=True)]
    psum x1 -> x0, waiting for transfers between devices: 22.4 us -> none  [body(): lax.psum(head_part.astype(jnp.bfloat16), 'group').astype(jnp.float32)]
    all_to_all x3 -> x0, starting transfers between devices: 14.7 us -> none  [the longest x1 7.24 us: body(): lax.all_to_all(outgoing, 'expert', split_axis=0, concat_axis=0, tiled=True)]
  transfers between devices with their start and end apart: 7 -> 0, of which waited for: 4 -> 0; matrix products, arithmetic and copies ran while one was open for 4% -> 0% of each run, Pallas kernels for 0% -> 0%
where the time goes in v1:
time: 139 us; the launch traced here: 138 us
  Pallas kernels  132 us (95%)
  local copies, waits for them, and re-layouts  3.47 us (2%)
  matrix products  2.2 us (2%)
    pallas_call x1, Pallas kernels, body(): pl.pallas_call(functools.partial(kernel, n, groups, gather_weights, n ==...  132 us
    unnamed x10, local copies, waits for them, and re-layouts  3.47 us

profile of v1, /device:TPU:0, one launch (start us, length us, event | category | flops | bytes accessed | tf_op | source)
XLA Modules:
  0.0 138.4 jit_solution(10977746127116158301)
XLA Ops:
  0.6 0.0 copy-start.1
  0.6 1.3 copy.15
  1.9 0.0 copy-done.1
  1.9 0.0 copy-start.2
  1.9 0.7 copy.11.ids_ref
  2.7 0.0 copy-done.2
  2.7 0.7 copy.12.score_ref
  3.4 132.1 %shard_map.104 = (bf16[128,1024]{1,0:T(8,128)(2,1)}, f32[2,8,1024]{2,1,0:T(8,128)}, f32[2,8,250]{2,1,0:T(8,128)}) custom-call(bf16[128,1024]{1,0:T(8,128)(2,1)} %tok_ref.1, s32[128,8]{1,0:T(8,128)} %copy.11.ids_ref, f32[128,8]{1,0:T(8,128)} %copy.12.score_ref, f32[1,1024]{1,0:T(1,128)} %bitcast.7, bf16[1024,250]{1,0:T(8,128)(2,1)} %head_ref.1, ...), custom_call_target="tpu_custom_call" | custom-call | tf_op jit(solution)/shard_map/pallas_call | solution.py:368
  135.5 0.0 copy-start
  135.5 2.2 %convolution_bitcast_fusion = f32[1024,250]{1,0:T(8,128)} fusion(f32[2,8,1024]{2,1,0:T(8,128)} %get-tuple-element.6, f32[2,8,250]{2,1,0:T(8,128)} %get-tuple-element.7), kind=kOutput, calls=%fused_computation | convolution fusion | flops 8212384 | bytes 1105536 | tf_op jit(solution)/shard_map/dot_general | solution.py:422
  137.7 0.0 copy-done
  137.7 0.7 copy.17
Async XLA Ops:
  0.6 1.3 copy-start.1
  1.9 0.7 copy-start.2
  135.5 2.2 %copy-start = (bf16[128,1024]{1,0:T(8,128)(2,1)S(1)}, bf16[128,1024]{1,0:T(8,128)(2,1)}, u32[]{:S(2)}) copy-start(bf16[128,1024]{1,0:T(8,128)(2,1)} %get-tuple-element.10) | copy-start | bytes 786436

commit v2 on v1

--- a/solution.py
+++ b/solution.py
@@ -112,26 +112,32 @@
 
     pl.semaphore_wait(barrier, n - 1 + groups - 1)
 
-    def cw(buf, phase, k):
+    piece = rows // 2
+
+    def chunk(buf, at, c):
+        return buf.at[(*at, pl.ds(c * piece, piece))]
+
+    def cw(buf, phase, k, c):
         return pltpu.make_async_remote_copy(
-            src_ref=buf.at[k],
-            dst_ref=buf.at[k + 1],
-            send_sem=cw_send.at[phase, k],
-            recv_sem=ring_recv.at[phase, k + 1],
+            src_ref=chunk(buf, (k,), c),
+            dst_ref=chunk(buf, (k + 1,), c),
+            send_sem=cw_send.at[phase, c, k],
+            recv_sem=ring_recv.at[phase, c, k + 1],
             device_id={"expert": right},
         )
 
-    def ccw(buf, phase, k):
+    def ccw(buf, phase, k, c):
         return pltpu.make_async_remote_copy(
-            src_ref=buf.at[lax.rem(k, n)],
-            dst_ref=buf.at[k - 1],
-            send_sem=ccw_send.at[phase, k - 1],
-            recv_sem=ring_recv.at[phase, k - 1],
+            src_ref=chunk(buf, (lax.rem(k, n),), c),
+            dst_ref=chunk(buf, (k - 1,), c),
+            send_sem=ccw_send.at[phase, c, k - 1],
+            recv_sem=ring_recv.at[phase, c, k - 1],
             device_id={"expert": left},
         )
 
-    cw(xbuf, 0, 0).start()
-    ccw(xbuf, 0, n).start()
+    for c in range(2):
+        cw(xbuf, 0, 0, c).start()
+        ccw(xbuf, 0, n, c).start()
 
     w_copies = []
     if gather_weights:
@@ -148,10 +154,12 @@
                 )
                 copy.start()
                 w_copies.append(copy)
-    for copy in locals_:
-        copy.wait()
-    for copy in w_copies:
-        copy.wait()
+
+    def weights_ready():
+        for copy in locals_:
+            copy.wait()
+        for copy in w_copies:
+            copy.wait()
 
     def forward_block(k):
         x = xbuf[k, :, :width]
@@ -181,103 +189,128 @@
             total += lax.dot_general(up_grad, wu[j], NT, preferred_element_type=jnp.float32)
         part[1, k] = total.astype(jnp.bfloat16)
 
-    def gather_phase(buf, phase, block):
+    def gather_phase(buf, phase, block, ready):
+        def arrive(s):
+            for c in range(2):
+                cw(buf, phase, s - 1, c).wait_recv()
+
+                @pl.when((s < half - 1) | (c == 0))
+                def _():
+                    cw(buf, phase, s, c).start()
+
+                ccw(buf, phase, n - s + 1, c).wait_recv()
+
+                @pl.when((s < half - 1) | (c == 1))
+                def _():
+                    ccw(buf, phase, n - s, c).start()
+
+        arrive(jnp.int32(1))
+        ready()
+
         def step(i, carry):
             s = (i + 1) // 2
             odd = lax.rem(i, 2)
 
-            @pl.when(odd == 1)
+            @pl.when((odd == 1) & (s > 1) & (s < half))
             def _():
-                cw(buf, phase, s - 1).wait_recv()
-
-                @pl.when(s < half)
-                def _():
-                    cw(buf, phase, s).start()
-                    ccw(buf, phase, n - s + 1).wait_recv()
-
-                    @pl.when(s < half - 1)
-                    def _():
-                        ccw(buf, phase, n - s).start()
+                arrive(s)
+
+            @pl.when((odd == 1) & (s == half))
+            def _():
+                cw(buf, phase, half - 1, 0).wait_recv()
+                ccw(buf, phase, half + 1, 1).wait_recv()
 
             block(odd * s + (1 - odd) * lax.rem(n - s, n))
             return carry
 
         lax.fori_loop(0, n, step, 0)
-
-        def drain_cw(k, carry):
-            cw(buf, phase, k).wait_send()
-            return carry
-
-        def drain_ccw(k, carry):
-            ccw(buf, phase, n - k).wait_send()
-            return carry
-
-        lax.fori_loop(0, half, drain_cw, 0)
-        lax.fori_loop(0, half - 1, drain_ccw, 0)
-
-    def to_left(phase, k):
+        for c in range(2):
+
+            def drain_cw(k, carry):
+                cw(buf, phase, k, c).wait_send()
+                return carry
+
+            def drain_ccw(k, carry):
+                ccw(buf, phase, n - k, c).wait_send()
+                return carry
+
+            lax.fori_loop(0, half - c, drain_cw, 0)
+            lax.fori_loop(0, half - 1 + c, drain_ccw, 0)
+
+    def to_left(phase, k, c):
         return pltpu.make_async_remote_copy(
-            src_ref=part.at[phase, k],
-            dst_ref=from_right.at[phase, k - 1],
-            send_sem=left_send.at[phase, k],
-            recv_sem=left_recv.at[phase, k - 1],
+            src_ref=chunk(part, (phase, k), c),
+            dst_ref=chunk(from_right, (phase, k - 1), c),
+            send_sem=left_send.at[phase, c, k],
+            recv_sem=left_recv.at[phase, c, k - 1],
             device_id={"expert": left},
         )
 
-    def to_right(phase, d):
+    def to_right(phase, d, c):
         return pltpu.make_async_remote_copy(
-            src_ref=part.at[phase, n - d],
-            dst_ref=from_left.at[phase, d - 1],
-            send_sem=right_send.at[phase, d],
-            recv_sem=right_recv.at[phase, d - 1],
+            src_ref=chunk(part, (phase, n - d), c),
+            dst_ref=chunk(from_left, (phase, d - 1), c),
+            send_sem=right_send.at[phase, c, d],
+            recv_sem=right_recv.at[phase, c, d - 1],
             device_id={"expert": right},
         )
 
+    def add_piece(phase, slot, incoming, at, c):
+        span = pl.ds(c * piece, piece)
+        part[phase, slot, span] = (
+            part[phase, slot, span].astype(jnp.float32)
+            + incoming[phase, at, span].astype(jnp.float32)
+        ).astype(jnp.bfloat16)
+
     def reduce_phase(phase):
-        to_left(phase, half).start()
-        to_right(phase, half - 1).start()
+        to_left(phase, half, 0).start()
+        to_right(phase, half, 1).start()
+        to_right(phase, half - 1, 0).start()
+        to_left(phase, half - 1, 1).start()
+
+        def pass_left(k, c):
+            to_left(phase, k + 1, c).wait_recv()
+            add_piece(phase, k, from_right, k, c)
+            to_left(phase, k, c).start()
+
+        def pass_right(d, c):
+            to_right(phase, d + 1, c).wait_recv()
+            add_piece(phase, n - d, from_left, d, c)
+            to_right(phase, d, c).start()
 
         def step(s, carry):
-            k = half - s
-            to_left(phase, k + 1).wait_recv()
-            part[phase, k] = (
-                part[phase, k].astype(jnp.float32) + from_right[phase, k].astype(jnp.float32)
-            ).astype(jnp.bfloat16)
-            to_left(phase, k).start()
+            pass_left(half - s, 0)
+            pass_right(half - s, 1)
 
             @pl.when(s < half - 1)
             def _():
-                d = half - 1 - s
-                to_right(phase, d + 1).wait_recv()
-                part[phase, n - d] = (
-                    part[phase, n - d].astype(jnp.float32)
-                    + from_left[phase, d].astype(jnp.float32)
-                ).astype(jnp.bfloat16)
-                to_right(phase, d).start()
+                pass_right(half - 1 - s, 0)
+                pass_left(half - 1 - s, 1)
 
             return carry
 
         lax.fori_loop(1, half, step, 0)
-        to_right(phase, 1).wait_recv()
-        to_left(phase, 1).wait_recv()
-
-        def drain_left(k, carry):
-            to_left(phase, k).wait_send()
-            return carry
-
-        def drain_right(d, carry):
-            to_right(phase, d).wait_send()
-            return carry
-
-        lax.fori_loop(1, half + 1, drain_left, 0)
-        lax.fori_loop(1, half, drain_right, 0)
+        for c in range(2):
+            to_right(phase, 1, c).wait_recv()
+            to_left(phase, 1, c).wait_recv()
+
+            def drain_left(k, carry):
+                to_left(phase, k, c).wait_send()
+                return carry
+
+            def drain_right(d, carry):
+                to_right(phase, d, c).wait_send()
+                return carry
+
+            lax.fori_loop(1, half + 1 - c, drain_left, 0)
+            lax.fori_loop(1, half + c, drain_right, 0)
         return (
             part[phase, 0].astype(jnp.float32)
             + from_right[phase, 0].astype(jnp.float32)
             + from_left[phase, 0].astype(jnp.float32)
         )
 
-    gather_phase(xbuf, 0, forward_block)
+    gather_phase(xbuf, 0, forward_block, weights_ready)
     residual = xbuf[0, :, :width].astype(jnp.float32) + reduce_phase(0)
     gain = gain_ref[...]
     inv_rms = lax.rsqrt(jnp.mean(residual * residual, axis=-1, keepdims=True) + NORM_EPS)
@@ -340,10 +373,11 @@
         cube * jnp.mean(residual * scaled, axis=-1, keepdims=True)
     )
     gbuf[0] = resid_grad.astype(jnp.bfloat16)
-    cw(gbuf, 1, 0).start()
-    ccw(gbuf, 1, n).start()
+    for c in range(2):
+        cw(gbuf, 1, 0, c).start()
+        ccw(gbuf, 1, n, c).start()
     resid[...] = resid_grad
-    gather_phase(gbuf, 1, backward_block)
+    gather_phase(gbuf, 1, backward_block, lambda: None)
     out_ref[...] = (resid[...] + reduce_phase(1)).astype(jnp.bfloat16)
     for copy in group_copies:
         copy.wait()
@@ -393,13 +427,13 @@
             dma((3,)),
             dma((groups, 3)),
             dma((groups, 3)),
-            dma((2, n)),
-            dma((2, n)),
-            dma((2, n)),
-            dma((2, n)),
-            dma((2, n)),
-            dma((2, n)),
-            dma((2, n)),
+            dma((2, 2, n)),
+            dma((2, 2, n)),
+            dma((2, 2, n)),
+            dma((2, 2, n)),
+            dma((2, 2, n)),
+            dma((2, 2, n)),
+            dma((2, 2, n)),
             dma((2, n)),
             dma((2, n)),
             dma((groups, 2)),

time: 139 us -> 118 us (0.85)
  Pallas kernels: 132 us -> 111 us
    pallas_call x1, Pallas kernels: 132 us -> 111 us  [body(): pl.pallas_call(functools.partial(kernel, n, groups, gather_weights, n ==...]
where the time goes in v2:
time: 118 us
  Pallas kernels  111 us (94%)
  local copies, waits for them, and re-layouts  3.47 us (3%)
  matrix products  2.2 us (2%)
    pallas_call x1, Pallas kernels, body(): pl.pallas_call(functools.partial(kernel, n, groups, gather_weights, n ==...  111 us
    unnamed x10, local copies, waits for them, and re-layouts  3.47 us

profile of v2, /device:TPU:0, one launch (start us, length us, event | category | flops | bytes accessed | tf_op | source)
XLA Modules:
  0.0 117.6 jit_solution(9776013164327482607)
XLA Ops:
  0.6 0.0 copy-start.1
  0.6 1.3 %copy.15 = s32[8,1,250]{2,0,1:T(8,128)} copy(s32[8,1,250]{2,1,0:T(1,128)} %param.17) | data formatting | bytes 16000
  1.9 0.0 copy-done.1
  1.9 0.0 copy-start.2
  1.9 0.7 copy.11.ids_ref
  2.7 0.0 copy-done.2
  2.7 0.7 copy.12.score_ref
  3.4 111.3 %shard_map.104 = (bf16[128,1024]{1,0:T(8,128)(2,1)}, f32[2,8,1024]{2,1,0:T(8,128)}, f32[2,8,250]{2,1,0:T(8,128)}) custom-call(bf16[128,1024]{1,0:T(8,128)(2,1)} %tok_ref.1, s32[128,8]{1,0:T(8,128)} %copy.11.ids_ref, f32[128,8]{1,0:T(8,128)} %copy.12.score_ref, f32[1,1024]{1,0:T(1,128)} %bitcast.7, bf16[1024,250]{1,0:T(8,128)(2,1)} %head_ref.1, ...), custom_call_target="tpu_custom_call" | custom-call | tf_op jit(solution)/shard_map/pallas_call | solution.py:402
  114.7 0.0 copy-start
  114.7 2.2 %convolution_bitcast_fusion = f32[1024,250]{1,0:T(8,128)} fusion(f32[2,8,1024]{2,1,0:T(8,128)} %get-tuple-element.6, f32[2,8,250]{2,1,0:T(8,128)} %get-tuple-element.7), kind=kOutput, calls=%fused_computation | convolution fusion | flops 8212384 | bytes 1105536 | tf_op jit(solution)/shard_map/dot_general | solution.py:456
  116.9 0.0 copy-done
  116.9 0.7 copy.17
Async XLA Ops:
  0.6 1.3 %copy-start.1 = (s32[128,8]{0,1:T(8,128)S(1)}, s32[128,8]{0,1:T(8,128)}, u32[]{:S(2)}) copy-start(s32[128,8]{0,1:T(8,128)} %param.13) | copy-start | bytes 12292
  1.9 0.7 copy-start.2
  114.7 2.2 %copy-start = (bf16[128,1024]{1,0:T(8,128)(2,1)S(1)}, bf16[128,1024]{1,0:T(8,128)(2,1)}, u32[]{:S(2)}) copy-start(bf16[128,1024]{1,0:T(8,128)(2,1)} %get-tuple-element.10) | copy-start | bytes 786436

commit v3 on v2

--- a/solution.py
+++ b/solution.py
@@ -112,7 +112,9 @@
 
     pl.semaphore_wait(barrier, n - 1 + groups - 1)
 
-    piece = rows // 2
+    pieces = 4
+    piece = rows // pieces
+    turn = pieces // 2
 
     def chunk(buf, at, c):
         return buf.at[(*at, pl.ds(c * piece, piece))]
@@ -135,7 +137,7 @@
             device_id={"expert": left},
         )
 
-    for c in range(2):
+    for c in range(pieces):
         cw(xbuf, 0, 0, c).start()
         ccw(xbuf, 0, n, c).start()
 
@@ -191,16 +193,16 @@
 
     def gather_phase(buf, phase, block, ready):
         def arrive(s):
-            for c in range(2):
+            for c in range(pieces):
                 cw(buf, phase, s - 1, c).wait_recv()
 
-                @pl.when((s < half - 1) | (c == 0))
+                @pl.when((s < half - 1) | (c < turn))
                 def _():
                     cw(buf, phase, s, c).start()
 
                 ccw(buf, phase, n - s + 1, c).wait_recv()
 
-                @pl.when((s < half - 1) | (c == 1))
+                @pl.when((s < half - 1) | (c >= turn))
                 def _():
                     ccw(buf, phase, n - s, c).start()
 
@@ -217,14 +219,15 @@
 
             @pl.when((odd == 1) & (s == half))
             def _():
-                cw(buf, phase, half - 1, 0).wait_recv()
-                ccw(buf, phase, half + 1, 1).wait_recv()
+                for c in range(turn):
+                    cw(buf, phase, half - 1, c).wait_recv()
+                    ccw(buf, phase, half + 1, c + turn).wait_recv()
 
             block(odd * s + (1 - odd) * lax.rem(n - s, n))
             return carry
 
         lax.fori_loop(0, n, step, 0)
-        for c in range(2):
+        for c in range(pieces):
 
             def drain_cw(k, carry):
                 cw(buf, phase, k, c).wait_send()
@@ -234,8 +237,8 @@
                 ccw(buf, phase, n - k, c).wait_send()
                 return carry
 
-            lax.fori_loop(0, half - c, drain_cw, 0)
-            lax.fori_loop(0, half - 1 + c, drain_ccw, 0)
+            lax.fori_loop(0, half - c // turn, drain_cw, 0)
+            lax.fori_loop(0, half - 1 + c // turn, drain_ccw, 0)
 
     def to_left(phase, k, c):
         return pltpu.make_async_remote_copy(
@@ -263,10 +266,12 @@
         ).astype(jnp.bfloat16)
 
     def reduce_phase(phase):
-        to_left(phase, half, 0).start()
-        to_right(phase, half, 1).start()
-        to_right(phase, half - 1, 0).start()
-        to_left(phase, half - 1, 1).start()
+        for c in range(turn):
+            to_left(phase, half, c).start()
+            to_right(phase, half, c + turn).start()
+        for c in range(turn):
+            to_right(phase, half - 1, c).start()
+            to_left(phase, half - 1, c + turn).start()
 
         def pass_left(k, c):
             to_left(phase, k + 1, c).wait_recv()
@@ -279,18 +284,20 @@
             to_right(phase, d, c).start()
 
         def step(s, carry):
-            pass_left(half - s, 0)
-            pass_right(half - s, 1)
+            for c in range(turn):
+                pass_left(half - s, c)
+                pass_right(half - s, c + turn)
 
             @pl.when(s < half - 1)
             def _():
-                pass_right(half - 1 - s, 0)
-                pass_left(half - 1 - s, 1)
+                for c in range(turn):
+                    pass_right(half - 1 - s, c)
+                    pass_left(half - 1 - s, c + turn)
 
             return carry
 
         lax.fori_loop(1, half, step, 0)
-        for c in range(2):
+        for c in range(pieces):
             to_right(phase, 1, c).wait_recv()
             to_left(phase, 1, c).wait_recv()
 
@@ -302,8 +309,8 @@
                 to_right(phase, d, c).wait_send()
                 return carry
 
-            lax.fori_loop(1, half + 1 - c, drain_left, 0)
-            lax.fori_loop(1, half + c, drain_right, 0)
+            lax.fori_loop(1, half + 1 - c // turn, drain_left, 0)
+            lax.fori_loop(1, half + c // turn, drain_right, 0)
         return (
             part[phase, 0].astype(jnp.float32)
             + from_right[phase, 0].astype(jnp.float32)
@@ -373,7 +380,7 @@
         cube * jnp.mean(residual * scaled, axis=-1, keepdims=True)
     )
     gbuf[0] = resid_grad.astype(jnp.bfloat16)
-    for c in range(2):
+    for c in range(pieces):
         cw(gbuf, 1, 0, c).start()
         ccw(gbuf, 1, n, c).start()
     resid[...] = resid_grad
@@ -427,13 +434,13 @@
             dma((3,)),
             dma((groups, 3)),
             dma((groups, 3)),
-            dma((2, 2, n)),
-            dma((2, 2, n)),
-            dma((2, 2, n)),
-            dma((2, 2, n)),
-            dma((2, 2, n)),
-            dma((2, 2, n)),
-            dma((2, 2, n)),
+            dma((2, 4, n)),
+            dma((2, 4, n)),
+            dma((2, 4, n)),
+            dma((2, 4, n)),
+            dma((2, 4, n)),
+            dma((2, 4, n)),
+            dma((2, 4, n)),
             dma((2, n)),
             dma((2, n)),
             dma((groups, 2)),

time: 118 us -> 115 us (0.975)
  Pallas kernels: 111 us -> 109 us
    pallas_call x1, Pallas kernels: 111 us -> 109 us  [body(): pl.pallas_call(functools.partial(kernel, n, groups, gather_weights, n ==...]
where the time goes in v3:
time: 115 us
  Pallas kernels  109 us (95%)
  local copies, waits for them, and re-layouts  3.47 us (3%)
  matrix products  2.2 us (2%)
    pallas_call x1, Pallas kernels, body(): pl.pallas_call(functools.partial(kernel, n, groups, gather_weights, n ==...  109 us
    unnamed x10, local copies, waits for them, and re-layouts  3.47 us

profile of v3, /device:TPU:0, one launch (start us, length us, event | category | flops | bytes accessed | tf_op | source)
XLA Modules:
  0.0 114.9 jit_solution(9579066952920432023)
XLA Ops:
  0.6 0.0 copy-start.1
  0.6 1.3 %copy.15 = s32[8,1,250]{2,0,1:T(8,128)} copy(s32[8,1,250]{2,1,0:T(1,128)} %param.17) | data formatting | bytes 16000
  1.9 0.0 copy-done.1
  1.9 0.0 copy-start.2
  1.9 0.7 copy.11.ids_ref
  2.7 0.0 copy-done.2
  2.7 0.7 copy.12.score_ref
  3.4 108.5 %shard_map.104 = (bf16[128,1024]{1,0:T(8,128)(2,1)}, f32[2,8,1024]{2,1,0:T(8,128)}, f32[2,8,250]{2,1,0:T(8,128)}) custom-call(bf16[128,1024]{1,0:T(8,128)(2,1)} %tok_ref.1, s32[128,8]{1,0:T(8,128)} %copy.11.ids_ref, f32[128,8]{1,0:T(8,128)} %copy.12.score_ref, f32[1,1024]{1,0:T(1,128)} %bitcast.7, bf16[1024,250]{1,0:T(8,128)(2,1)} %head_ref.1, ...), custom_call_target="tpu_custom_call" | custom-call | tf_op jit(solution)/shard_map/pallas_call | solution.py:409
  111.9 0.0 copy-start
  112.0 2.2 %convolution_bitcast_fusion = f32[1024,250]{1,0:T(8,128)} fusion(f32[2,8,1024]{2,1,0:T(8,128)} %get-tuple-element.6, f32[2,8,250]{2,1,0:T(8,128)} %get-tuple-element.7), kind=kOutput, calls=%fused_computation | convolution fusion | flops 8212384 | bytes 1105536 | tf_op jit(solution)/shard_map/dot_general | solution.py:463
  114.1 0.0 copy-done
  114.1 0.7 copy.17
Async XLA Ops:
  0.6 1.3 %copy-start.1 = (s32[128,8]{0,1:T(8,128)S(1)}, s32[128,8]{0,1:T(8,128)}, u32[]{:S(2)}) copy-start(s32[128,8]{0,1:T(8,128)} %param.13) | copy-start | bytes 12292
  1.9 0.7 copy-start.2
  111.9 2.2 %copy-start = (bf16[128,1024]{1,0:T(8,128)(2,1)S(1)}, bf16[128,1024]{1,0:T(8,128)(2,1)}, u32[]{:S(2)}) copy-start(bf16[128,1024]{1,0:T(8,128)(2,1)} %get-tuple-element.10) | copy-start | bytes 786436

commit v4 on v3

--- a/solution.py
+++ b/solution.py
@@ -60,6 +60,8 @@
     pool_all,
     terms,
     terms_in,
+    grad_mine,
+    pool_grads,
     w_local_sem,
     w_send_sem,
     w_recv_sem,
@@ -180,8 +182,17 @@
             )
         part[0, k] = total.astype(jnp.bfloat16)
 
+    def residual_gradient(residual, pooled_grad):
+        inv_rms = lax.rsqrt(jnp.mean(residual * residual, axis=-1, keepdims=True) + NORM_EPS)
+        scaled = gain_ref[...] * pooled_grad / rows
+        cube = inv_rms * inv_rms * inv_rms
+        return inv_rms * scaled - residual * (
+            cube * jnp.mean(residual * scaled, axis=-1, keepdims=True)
+        )
+
     def backward_block(k):
-        g = gbuf[k]
+        source = ring_expert(lax.rem(place - k + n, n), n, snake)
+        g = residual_gradient(gbuf[k].astype(jnp.float32), pool_grads[source]).astype(jnp.bfloat16)
         total = jnp.zeros((rows, width), jnp.float32)
         for j in range(local):
             back = lax.dot_general(g, wd[j], NT, preferred_element_type=jnp.float32)
@@ -206,16 +217,18 @@
                 def _():
                     ccw(buf, phase, n - s, c).start()
 
-        arrive(jnp.int32(1))
-        ready()
+        lead = len(ready) - 1
+        for at, action in enumerate(ready):
+            arrive(jnp.int32(at + 1))
+            action()
 
         def step(i, carry):
             s = (i + 1) // 2
             odd = lax.rem(i, 2)
 
-            @pl.when((odd == 1) & (s > 1) & (s < half))
+            @pl.when((odd == 1) & (s > 1) & (s + lead < half))
             def _():
-                arrive(s)
+                arrive(s + lead)
 
             @pl.when((odd == 1) & (s == half))
             def _():
@@ -317,11 +330,12 @@
             + from_left[phase, 0].astype(jnp.float32)
         )
 
-    gather_phase(xbuf, 0, forward_block, weights_ready)
+    gather_phase(xbuf, 0, forward_block, [weights_ready])
     residual = xbuf[0, :, :width].astype(jnp.float32) + reduce_phase(0)
     gain = gain_ref[...]
     inv_rms = lax.rsqrt(jnp.mean(residual * residual, axis=-1, keepdims=True) + NORM_EPS)
     resid[...] = residual
+    gbuf[0] = residual.astype(jnp.bfloat16)
     pooled = jnp.sum(residual * inv_rms * gain, axis=0, keepdims=True) / rows
     pooled = pooled.astype(jnp.bfloat16).astype(jnp.float32)
     pool_mine[...] = pooled
@@ -339,6 +353,9 @@
     copies = [small(0, pool_mine, pool_all.at[expert], off) for off in range(1, n)]
     for copy in copies:
         copy.start()
+    for c in range(pieces):
+        cw(gbuf, 1, 0, c).start()
+        ccw(gbuf, 1, n, c).start()
     for copy in copies:
         copy.wait()
     pooled_rows = jnp.concatenate([pool_all[i] for i in range(n)], axis=0).astype(jnp.bfloat16)
@@ -367,24 +384,25 @@
             )
             copy.start()
             group_copies.append(copy)
-    for copy in copies:
-        copy.wait()
-    pooled_grad = terms[expert]
-    for off in range(1, n):
-        pooled_grad = pooled_grad + terms_in[off]
-    residual = resid[...]
-    inv_rms = lax.rsqrt(jnp.mean(residual * residual, axis=-1, keepdims=True) + NORM_EPS)
-    scaled = gain * pooled_grad / rows
-    cube = inv_rms * inv_rms * inv_rms
-    resid_grad = inv_rms * scaled - residual * (
-        cube * jnp.mean(residual * scaled, axis=-1, keepdims=True)
-    )
-    gbuf[0] = resid_grad.astype(jnp.bfloat16)
-    for c in range(pieces):
-        cw(gbuf, 1, 0, c).start()
-        ccw(gbuf, 1, n, c).start()
-    resid[...] = resid_grad
-    gather_phase(gbuf, 1, backward_block, lambda: None)
+    grad_copies = [small(2, grad_mine, pool_grads.at[expert], off) for off in range(1, n)]
+
+    def send_pooled_grad():
+        for copy in copies:
+            copy.wait()
+        pooled_grad = terms[expert]
+        for off in range(1, n):
+            pooled_grad = pooled_grad + terms_in[off]
+        grad_mine[...] = pooled_grad
+        pool_grads[pl.ds(expert, 1)] = pooled_grad[None]
+        for copy in grad_copies:
+            copy.start()
+        resid[...] = residual_gradient(resid[...], pooled_grad)
+
+    def pooled_grads_ready():
+        for copy in grad_copies:
+            copy.wait()
+
+    gather_phase(gbuf, 1, backward_block, [send_pooled_grad, pooled_grads_ready])
     out_ref[...] = (resid[...] + reduce_phase(1)).astype(jnp.bfloat16)
     for copy in group_copies:
         copy.wait()
@@ -431,6 +449,8 @@
             pltpu.VMEM((n, 1, width), f32),
             pltpu.VMEM((n, 1, width), f32),
             pltpu.VMEM((n, 1, width), f32),
+            pltpu.VMEM((1, width), f32),
+            pltpu.VMEM((n, 1, width), f32),
             dma((3,)),
             dma((groups, 3)),
             dma((groups, 3)),
@@ -441,8 +461,8 @@
             dma((2, 4, n)),
             dma((2, 4, n)),
             dma((2, 4, n)),
-            dma((2, n)),
-            dma((2, n)),
+            dma((3, n)),
+            dma((3, n)),
             dma((groups, 2)),
             dma((groups, 2)),
         ],

time: 115 us -> 114 us (level)
  Pallas kernels: 109 us -> 107 us
    pallas_call x1, Pallas kernels: 109 us -> 107 us  [body(): pl.pallas_call(functools.partial(kernel, n, groups, gather_weights, n ==...]
where the time goes in v4:
time: 114 us; the launch traced here: 113 us
  Pallas kernels  107 us (94%)
  local copies, waits for them, and re-layouts  3.47 us (3%)
  matrix products  2.2 us (2%)
    pallas_call x1, Pallas kernels, body(): pl.pallas_call(functools.partial(kernel, n, groups, gather_weights, n ==...  107 us
    unnamed x10, local copies, waits for them, and re-layouts  3.47 us

profile of v4, /device:TPU:0, one launch (start us, length us, event | category | flops | bytes accessed | tf_op | source)
XLA Modules:
  0.0 113.5 jit_solution(11568284234447601041)
XLA Ops:
  0.6 0.0 copy-start.1
  0.6 1.3 %copy.15 = s32[8,1,250]{2,0,1:T(8,128)} copy(s32[8,1,250]{2,1,0:T(1,128)} %param.17) | data formatting | bytes 16000
  1.9 0.0 copy-done.1
  1.9 0.0 copy-start.2
  1.9 0.7 copy.11.ids_ref
  2.7 0.0 copy-done.2
  2.7 0.7 copy.12.score_ref
  3.4 107.1 %shard_map.104 = (bf16[128,1024]{1,0:T(8,128)(2,1)}, f32[2,8,1024]{2,1,0:T(8,128)}, f32[2,8,250]{2,1,0:T(8,128)}) custom-call(bf16[128,1024]{1,0:T(8,128)(2,1)} %tok_ref.1, s32[128,8]{1,0:T(8,128)} %copy.11.ids_ref, f32[128,8]{1,0:T(8,128)} %copy.12.score_ref, f32[1,1024]{1,0:T(1,128)} %bitcast.7, bf16[1024,250]{1,0:T(8,128)(2,1)} %head_ref.1, ...), custom_call_target="tpu_custom_call" | custom-call | tf_op jit(solution)/shard_map/pallas_call | solution.py:427
  110.5 0.0 copy-start
  110.5 2.2 %convolution_bitcast_fusion = f32[1024,250]{1,0:T(8,128)} fusion(f32[2,8,1024]{2,1,0:T(8,128)} %get-tuple-element.6, f32[2,8,250]{2,1,0:T(8,128)} %get-tuple-element.7), kind=kOutput, calls=%fused_computation | convolution fusion | flops 8212384 | bytes 1105536 | tf_op jit(solution)/shard_map/dot_general | solution.py:483
  112.7 0.0 copy-done
  112.8 0.7 copy.17
Async XLA Ops:
  0.6 1.3 %copy-start.1 = (s32[128,8]{0,1:T(8,128)S(1)}, s32[128,8]{0,1:T(8,128)}, u32[]{:S(2)}) copy-start(s32[128,8]{0,1:T(8,128)} %param.13) | copy-start | bytes 12292
  1.9 0.7 copy-start.2
  110.5 2.2 %copy-start = (bf16[128,1024]{1,0:T(8,128)(2,1)S(1)}, bf16[128,1024]{1,0:T(8,128)(2,1)}, u32[]{:S(2)}) copy-start(bf16[128,1024]{1,0:T(8,128)(2,1)} %get-tuple-element.10) | copy-start | bytes 786436

commit v5 on v4

--- a/solution.py
+++ b/solution.py
@@ -102,12 +102,14 @@
 
     ids = ids_ref[...]
     score = score_ref[...]
-    weight = score / jnp.sum(score, axis=-1, keepdims=True)
+    weight = score / jnp.sum(score, axis=0, keepdims=True)
     lane = lax.rem(lax.broadcasted_iota(jnp.int32, (rows, LANES), 1), HALF)
     low = lax.broadcasted_iota(jnp.int32, (rows, LANES), 1) < HALF
-    by_expert = jnp.zeros((rows, LANES), jnp.float32)
-    for k in range(ids.shape[1]):
-        by_expert += jnp.where(lane == ids[:, k : k + 1], weight[:, k : k + 1], 0.0)
+    named = lax.rem(lax.broadcasted_iota(jnp.int32, (LANES, rows), 0), HALF)
+    by_expert = jnp.zeros((LANES, rows), jnp.float32)
+    for k in range(ids.shape[0]):
+        by_expert += jnp.where(named == ids[k : k + 1, :], weight[k : k + 1, :], 0.0)
+    by_expert = by_expert.T
     high_part = by_expert.astype(jnp.bfloat16).astype(jnp.float32)
     xbuf[0, :, :width] = tok_ref[...]
     xbuf[0, :, width:] = jnp.where(low, high_part, by_expert - high_part).astype(jnp.bfloat16)
@@ -237,6 +239,13 @@
                     ccw(buf, phase, half + 1, c + turn).wait_recv()
 
             block(odd * s + (1 - odd) * lax.rem(n - s, n))
+
+            @pl.when(i == n - 2)
+            def _():
+                for c in range(turn):
+                    to_right(phase, half - 1, c).start()
+                    to_left(phase, half - 1, c + turn).start()
+
             return carry
 
         lax.fori_loop(0, n, step, 0)
@@ -282,9 +291,6 @@
         for c in range(turn):
             to_left(phase, half, c).start()
             to_right(phase, half, c + turn).start()
-        for c in range(turn):
-            to_right(phase, half - 1, c).start()
-            to_left(phase, half - 1, c + turn).start()
 
         def pass_left(k, c):
             to_left(phase, k + 1, c).wait_recv()
@@ -360,8 +366,9 @@
         copy.wait()
     pooled_rows = jnp.concatenate([pool_all[i] for i in range(n)], axis=0).astype(jnp.bfloat16)
     logits = jnp.dot(pooled_rows, head_ref[...], preferred_element_type=jnp.float32)
+    target_rows = jnp.concatenate([target_ref[i] for i in range(n)], axis=0)
     sig = 1.0 / (1.0 + jnp.exp(-logits))
-    logit_grad = (LOSS_SCALE * (sig - target_ref[...].astype(jnp.float32))).astype(jnp.bfloat16)
+    logit_grad = (LOSS_SCALE * (sig - target_rows.astype(jnp.float32))).astype(jnp.bfloat16)
     pooled_terms = lax.dot_general(logit_grad, head_ref[...], NT, preferred_element_type=jnp.float32)
     for i in range(n):
         terms[i] = pooled_terms[i : i + 1, :]
@@ -471,11 +478,11 @@
         ),
     )(
         tokens,
-        route_ids,
-        route_scores,
+        route_ids.T,
+        route_scores.T,
         norm_gain.reshape(1, width),
         class_head,
-        targets.reshape(n, labels),
+        targets,
         w_gate,
         w_up,
         w_down,

time: 114 us -> 110 us (0.965)
  local copies, waits for them, and re-layouts: 3.47 us -> 0.71 us
    unnamed x10 -> x3, local copies, waits for them, and re-layouts: 3.47 us -> 0.71 us
where the time goes in v5:
time: 110 us
  Pallas kernels  107 us (97%)
  matrix products  2.2 us (2%)
    pallas_call x1, Pallas kernels, body(): pl.pallas_call(functools.partial(kernel, n, groups, gather_weights, n ==...  107 us

profile of v5, /device:TPU:0, one launch (start us, length us, event | category | flops | bytes accessed | tf_op | source)
XLA Modules:
  0.0 110.1 jit_solution(6167922615843567593)
XLA Ops:
  0.6 106.6 %shard_map.104 = (bf16[128,1024]{1,0:T(8,128)(2,1)}, f32[2,8,1024]{2,1,0:T(8,128)}, f32[2,8,250]{2,1,0:T(8,128)}) custom-call(bf16[128,1024]{1,0:T(8,128)(2,1)} %tok_ref.1, s32[8,128]{1,0:T(8,128)} %bitcast.5, f32[8,128]{1,0:T(8,128)} %bitcast.6, f32[1,1024]{1,0:T(1,128)} %bitcast.7, bf16[1024,250]{1,0:T(8,128)(2,1)} %head_ref.1, s32[8,1,250]{2,1,0:T(1,128)} %target_ref.1, ...), custom_call_target="tpu_custom_call" | custom-call | tf_op jit(solution)/shard_map/pallas_call | solution.py:434
  107.2 0.0 copy-start
  107.2 2.2 %convolution_bitcast_fusion = f32[1024,250]{1,0:T(8,128)} fusion(f32[2,8,1024]{2,1,0:T(8,128)} %get-tuple-element.6, f32[2,8,250]{2,1,0:T(8,128)} %get-tuple-element.7), kind=kOutput, calls=%fused_computation | convolution fusion | flops 8212384 | bytes 1105536 | tf_op jit(solution)/shard_map/dot_general | solution.py:490
  109.4 0.0 copy-done
  109.4 0.7 copy.12
Async XLA Ops:
  107.2 2.2 %copy-start = (bf16[128,1024]{1,0:T(8,128)(2,1)S(1)}, bf16[128,1024]{1,0:T(8,128)(2,1)}, u32[]{:S(2)}) copy-start(bf16[128,1024]{1,0:T(8,128)(2,1)} %get-tuple-element.10) | copy-start | bytes 786436

commit v6 on v5

--- a/solution.py
+++ b/solution.py
@@ -167,22 +167,29 @@
         for copy in w_copies:
             copy.wait()
 
-    def forward_block(k):
-        x = xbuf[k, :, :width]
-        ext = xbuf[k, :, width:].astype(jnp.float32)
-        total = jnp.zeros((rows, width), jnp.float32)
+    def stacked(values):
+        return jnp.concatenate(values, axis=0) if len(values) > 1 else values[0]
+
+    def forward_block(slots):
+        x = stacked([xbuf[k, :, :width] for k in slots])
+        exts = [xbuf[k, :, width:].astype(jnp.float32) for k in slots]
+        total = jnp.zeros(x.shape, jnp.float32)
         for j in range(local):
-            w = jnp.sum(jnp.where(lane == expert * local + j, ext, 0.0), axis=1, keepdims=True)
+            mine = lane == expert * local + j
+            w = stacked([jnp.sum(jnp.where(mine, e, 0.0), axis=1, keepdims=True) for e in exts])
             gate = jnp.dot(x, wg[j], preferred_element_type=jnp.float32)
             up = jnp.dot(x, wu[j], preferred_element_type=jnp.float32)
             sig = 1.0 / (1.0 + jnp.exp(-gate))
             silu = gate * sig * w
-            gate_coef[k, j] = up * (sig * (1.0 + gate * (1.0 - sig))) * w
-            up_coef[k, j] = silu
+            slope = up * (sig * (1.0 + gate * (1.0 - sig))) * w
+            for at, k in enumerate(slots):
+                gate_coef[k, j] = slope[at * rows : (at + 1) * rows]
+                up_coef[k, j] = silu[at * rows : (at + 1) * rows]
             total += jnp.dot(
                 (silu * up).astype(jnp.bfloat16), wd[j], preferred_element_type=jnp.float32
             )
-        part[0, k] = total.astype(jnp.bfloat16)
+        for at, k in enumerate(slots):
+            part[0, k] = total[at * rows : (at + 1) * rows].astype(jnp.bfloat16)
 
     def residual_gradient(residual, pooled_grad):
         inv_rms = lax.rsqrt(jnp.mean(residual * residual, axis=-1, keepdims=True) + NORM_EPS)
@@ -192,17 +199,22 @@
             cube * jnp.mean(residual * scaled, axis=-1, keepdims=True)
         )
 
-    def backward_block(k):
-        source = ring_expert(lax.rem(place - k + n, n), n, snake)
-        g = residual_gradient(gbuf[k].astype(jnp.float32), pool_grads[source]).astype(jnp.bfloat16)
-        total = jnp.zeros((rows, width), jnp.float32)
+    def backward_block(slots):
+        grads = []
+        for k in slots:
+            source = ring_expert(lax.rem(place - k + n, n), n, snake)
+            grad = residual_gradient(gbuf[k].astype(jnp.float32), pool_grads[source])
+            grads.append(grad.astype(jnp.bfloat16))
+        g = stacked(grads)
+        total = jnp.zeros(g.shape, jnp.float32)
         for j in range(local):
             back = lax.dot_general(g, wd[j], NT, preferred_element_type=jnp.float32)
-            gate_grad = (back * gate_coef[k, j]).astype(jnp.bfloat16)
-            up_grad = (back * up_coef[k, j]).astype(jnp.bfloat16)
+            gate_grad = (back * stacked([gate_coef[k, j] for k in slots])).astype(jnp.bfloat16)
+            up_grad = (back * stacked([up_coef[k, j] for k in slots])).astype(jnp.bfloat16)
             total += lax.dot_general(gate_grad, wg[j], NT, preferred_element_type=jnp.float32)
             total += lax.dot_general(up_grad, wu[j], NT, preferred_element_type=jnp.float32)
-        part[1, k] = total.astype(jnp.bfloat16)
+        for at, k in enumerate(slots):
+            part[1, k] = total[at * rows : (at + 1) * rows].astype(jnp.bfloat16)
 
     def gather_phase(buf, phase, block, ready):
         def arrive(s):
@@ -224,31 +236,24 @@
             arrive(jnp.int32(at + 1))
             action()
 
-        def step(i, carry):
-            s = (i + 1) // 2
-            odd = lax.rem(i, 2)
-
-            @pl.when((odd == 1) & (s > 1) & (s + lead < half))
+        block((0,))
+
+        def step(s, carry):
+            @pl.when((s > 1) & (s + lead < half))
             def _():
                 arrive(s + lead)
 
-            @pl.when((odd == 1) & (s == half))
-            def _():
-                for c in range(turn):
-                    cw(buf, phase, half - 1, c).wait_recv()
-                    ccw(buf, phase, half + 1, c + turn).wait_recv()
-
-            block(odd * s + (1 - odd) * lax.rem(n - s, n))
-
-            @pl.when(i == n - 2)
-            def _():
-                for c in range(turn):
-                    to_right(phase, half - 1, c).start()
-                    to_left(phase, half - 1, c + turn).start()
-
+            block((s, n - s))
             return carry
 
-        lax.fori_loop(0, n, step, 0)
+        lax.fori_loop(1, half, step, 0)
+        for c in range(turn):
+            to_right(phase, half - 1, c).start()
+            to_left(phase, half - 1, c + turn).start()
+        for c in range(turn):
+            cw(buf, phase, half - 1, c).wait_recv()
+            ccw(buf, phase, half + 1, c + turn).wait_recv()
+        block((half,))
         for c in range(pieces):
 
             def drain_cw(k, carry):

time: 110 us -> 106 us (0.964)
  Pallas kernels: 107 us -> 102 us
    pallas_call x1, Pallas kernels: 107 us -> 102 us  [body(): pl.pallas_call(functools.partial(kernel, n, groups, gather_weights, n ==...]
where the time goes in v6:
time: 106 us
  Pallas kernels  102 us (96%)
  matrix products  2.19 us (2%)
    pallas_call x1, Pallas kernels, body(): pl.pallas_call(functools.partial(kernel, n, groups, gather_weights, n ==...  102 us
    dot_general x1, matrix products, body(): lax.dot_general(pool.reshape(-1, width).astype(bf16), lg.reshape(-1, labe...  2.19 us

profile of v6, /device:TPU:0, one launch (start us, length us, event | category | flops | bytes accessed | tf_op | source)
XLA Modules:
  0.0 105.7 jit_solution(17452737261812608099)
XLA Ops:
  0.6 102.2 %shard_map.104 = (bf16[128,1024]{1,0:T(8,128)(2,1)}, f32[2,8,1024]{2,1,0:T(8,128)}, f32[2,8,250]{2,1,0:T(8,128)}) custom-call(bf16[128,1024]{1,0:T(8,128)(2,1)} %tok_ref.1, s32[8,128]{1,0:T(8,128)} %bitcast.5, f32[8,128]{1,0:T(8,128)} %bitcast.6, f32[1,1024]{1,0:T(1,128)} %bitcast.7, bf16[1024,250]{1,0:T(8,128)(2,1)} %head_ref.1, s32[8,1,250]{2,1,0:T(1,128)} %target_ref.1, ...), custom_call_target="tpu_custom_call" | custom-call | tf_op jit(solution)/shard_map/pallas_call | solution.py:439
  102.8 0.0 copy-start
  102.8 2.2 %convolution_bitcast_fusion = f32[1024,250]{1,0:T(8,128)} fusion(f32[2,8,1024]{2,1,0:T(8,128)} %get-tuple-element.6, f32[2,8,250]{2,1,0:T(8,128)} %get-tuple-element.7), kind=kOutput, calls=%fused_computation | convolution fusion | flops 8212384 | bytes 1105536 | tf_op jit(solution)/shard_map/dot_general | solution.py:495
  105.0 0.0 copy-done
  105.0 0.7 copy.12
Async XLA Ops:
  102.8 2.2 %copy-start = (bf16[128,1024]{1,0:T(8,128)(2,1)S(1)}, bf16[128,1024]{1,0:T(8,128)(2,1)}, u32[]{:S(2)}) copy-start(bf16[128,1024]{1,0:T(8,128)(2,1)} %get-tuple-element.10) | copy-start | bytes 786436
